TPU v7x, 32 devices: a whole 2x2x4 slice. The times are simulated.
32 devices in a mesh: req: 4 (over z), tile: 2 (over y), span: 4 (over x, core).
Axes of the slice: x: 2, y: 2, z: 4, core: 2. Of those that a mesh axis runs over, the one named last changes fastest.
Arguments:
- latents: bfloat16 [32, 16, 128, 512], P(('req', 'span'), 'tile'), may hold values from -12 to 12
- frame_counts: int32 [4], replicated, may hold values from 1 to 16, 32 in all
- norm_gain: float32 [512], replicated, may hold values from 0.1 to 1.9
- norm_shift: float32 [512], replicated, may hold values from -3 to 3
- conv_weight: bfloat16 [3, 3, 3, 512, 512], replicated, may hold values from -0.0546875 to 0.0546875
- conv_bias: float32 [512], replicated, may hold values from -2 to 2
Outputs:
- decoded: bfloat16 [32, 16, 128, 512], P(('req', 'span'), 'tile')
Inputs may be any that keep to these rules, and one draw needn't show every extreme that they name: `frame_counts`: the 4 counts sum to 32, and the largest is exactly 16.
All inputs are finite; a program needn't handle non-finite values.
Results may differ from a plain program's by a relative error of at most 0.0031.
Values may be sent and summed in bfloat16 or wider, within the bound.
A program may use at most 192 MiB of HBM per device.

v0:
```python
import jax
import jax.numpy as jnp
from jax import lax
from jax.sharding import PartitionSpec as P

GROUPS = 32


EPSILON = 1e-06


def extended_2(array, sides, width):
    for axis, dim in sides:
        count, length = (lax.axis_size(axis), array.shape[dim])
        up = [(i, (i + 1) % count) for i in range(count - 1)]
        down = [(j, i) for i, j in up]
        last = lax.slice_in_dim(array, length - width, length, axis=dim)
        leading = lax.slice_in_dim(array, 0, width, axis=dim)
        before = lax.ppermute(last, axis, up)
        after = lax.ppermute(leading, axis, down)
        array = jnp.concatenate([before, array, after], axis=dim)
    return array


def shifted(array, axis, by):
    count = lax.axis_size(axis)
    pairs = [(i, i + by) for i in range(count) if 0 <= i + by < count]
    return lax.ppermute(array, axis, pairs)


def membership(positions, request_start, request_end):
    return (positions[:, None] >= request_start[None, :]) & (
        positions[:, None] < request_end[None, :]
    )


def normalize(
    source, positions, request_start, request_end, group_mean, group_scale, norm_gain, norm_shift
):
    inside = membership(positions, request_start, request_end).astype(jnp.float32)
    per_group = source.shape[-1] // group_mean.shape[1]
    frame_mean = jnp.repeat(
        jnp.dot(inside, group_mean, precision=lax.Precision.HIGHEST), per_group, axis=1
    )
    frame_scale = jnp.repeat(
        jnp.dot(inside, group_scale, precision=lax.Precision.HIGHEST), per_group, axis=1
    )
    centred = (source.astype(jnp.float32) - frame_mean[:, None, None, :]) * frame_scale[
        :, None, None, :
    ]
    return jax.nn.silu(centred * norm_gain + norm_shift).astype(jnp.bfloat16)


def finish_stats(local_sums, local_squares, cell_count):
    total_sums, total_squares = lax.psum((local_sums, local_squares), ("req", "tile", "span"))
    group_mean = total_sums / cell_count
    group_scale = lax.rsqrt(total_squares / cell_count - group_mean * group_mean + EPSILON)
    return (group_mean, group_scale)


def extend_rows(source):
    haloed = extended_2(source, (("tile", 1),), 1)
    tile_place = lax.axis_index("tile")
    upper_rim = jnp.where(tile_place == 0, haloed[:, 1:2], haloed[:, 0:1])
    bottom = jnp.where(tile_place == lax.axis_size("tile") - 1, haloed[:, -2:-1], haloed[:, -1:])
    return jnp.concatenate([upper_rim, haloed[:, 1:-1], bottom], axis=1)


def extend_frames(source):
    earlier = shifted(source, ("req", "span"), 1)
    return jnp.concatenate([earlier, source], axis=0)


def extend(source):
    grown = extend_rows(extend_frames(source))
    return grown


def convolve(padded, tap_index, conv_weight, frame_count, row_count, col_count, channels):
    accumulated = jnp.zeros((frame_count * row_count * col_count, channels), jnp.float32)
    for time_tap in range(3):
        chosen = jnp.take(padded, tap_index[time_tap], axis=0)
        for row_tap in range(3):
            stacked = jnp.concatenate(
                [
                    chosen[:, row_tap : row_tap + row_count, col_tap : col_tap + col_count]
                    for col_tap in range(3)
                ],
                axis=-1,
            )
            kernel = conv_weight[time_tap, row_tap].reshape(3 * channels, channels)
            accumulated = accumulated + jnp.dot(
                stacked.reshape(frame_count * row_count * col_count, 3 * channels),
                kernel,
                preferred_element_type=jnp.float32,
            )
    return accumulated.reshape(frame_count, row_count, col_count, channels)


def shards(latents, frame_counts, norm_gain, norm_shift, conv_weight, conv_bias):
    frame_count, row_count, col_count, channels = latents.shape
    per_group = channels // GROUPS
    request_end = jnp.cumsum(frame_counts)
    request_start = request_end - frame_counts
    first_frame = lax.axis_index(("req", "span")) * frame_count
    positions = first_frame + jnp.arange(frame_count, dtype=jnp.int32)
    inside = membership(positions, request_start, request_end)
    values = latents.astype(jnp.float32)
    group_sums = jnp.sum(values, axis=(1, 2)).reshape(frame_count, GROUPS, per_group).sum(-1)
    group_squares = (
        jnp.sum(values * values, axis=(1, 2)).reshape(frame_count, GROUPS, per_group).sum(-1)
    )
    weights_in = inside.astype(jnp.float32)
    local_sums = jnp.dot(weights_in.T, group_sums, precision=lax.Precision.HIGHEST)
    local_squares = jnp.dot(weights_in.T, group_squares, precision=lax.Precision.HIGHEST)
    cell_count = (
        frame_counts * (row_count * lax.axis_size("tile") * col_count * per_group)
    ).astype(jnp.float32)[:, None]
    extended_raw = extend(latents)
    group_mean, group_scale = finish_stats(local_sums, local_squares, cell_count)
    extended_positions = first_frame - 2 + jnp.arange(frame_count + 2, dtype=jnp.int32)
    extended = normalize(
        extended_raw,
        extended_positions,
        request_start,
        request_end,
        group_mean,
        group_scale,
        norm_gain,
        norm_shift,
    )
    padded = jnp.pad(extended, ((0, 0), (0, 0), (1, 1), (0, 0)), mode="edge")
    frame_start = jnp.sum(jnp.where(inside, request_start[None, :], 0), axis=1)
    tap_index = jnp.stack(
        [
            jnp.maximum(positions - 2 + time_tap, frame_start) - first_frame + 2
            for time_tap in range(3)
        ],
        axis=0,
    )
    conv = convolve(padded, tap_index, conv_weight, frame_count, row_count, col_count, channels)
    return (values + conv + conv_bias).astype(jnp.bfloat16)


def solution(mesh):
    placed = (P(("req", "span"), "tile", None, None), P(), P(), P(), P(), P())
    return jax.shard_map(
        shards,
        mesh=mesh,
        in_specs=placed,
        out_specs=P(("req", "span"), "tile", None, None),
        check_vma=False,
    )
```

profile of v0, /device:TPU:1, one launch (start us, length us, event | category | flops | bytes accessed | tf_op | source)
XLA Modules:
  0.0 218.8 jit_solution(12181268029318585287)
XLA Ops:
  0.0 4.6 %collective-permute-start = (bf16[2,8,128,512]{3,2,1,0:T(8,128)(2,1)}, bf16[2,8,128,512]{3,2,1,0:T(8,128)(2,1)}, u32[]{:S(2)}, u32[]{:S(2)}) collective-permute-start(bf16[2,8,128,512]{3,2,1,0:T(8,128)(2,1)} %param.8), channel_id=1, source_target_pairs={{0,1},{1,2},{2,3},{3,8},{8,9},{9,10},{10,11},{11,16},{16,17},{17,1... | collective-permute-start | bytes 6291464 | tf_op jit(solution)/shard_map/ppermute | solution.py:28
  4.6 2.2 convert_reduce_fusion
  9.2 53.6 %all-reduce = (f32[4,32]{1,0:T(4,128)S(1)}, f32[4,32]{1,0:T(4,128)S(1)}) all-reduce(f32[4,32]{1,0:T(4,128)S(1)} %fusion.17, f32[4,32]{1,0:T(4,128)S(1)} %fusion.16), channel_id=1, replica_groups=mesh['req'=4,'tile'=2,'span'=4] {'req','tile','span'}, use_global_device_ids=true, to_apply=%region_6.7 | all-reduce | flops 256 | bytes 2048 | tf_op jit(solution)/shard_map/psum | solution.py:55
  63.6 1.8 constant_dynamic-update-slice_fusion.1
  65.7 3.1 %collective-permute-start.1 = (bf16[4,1,128,512]{3,2,1,0:T(8,128)(2,1)S(1)}, bf16[4,1,128,512]{3,2,1,0:T(8,128)(2,1)S(1)}, u32[]{:S(2)}, u32[]{:S(2)}) collective-permute-start(bf16[4,1,128,512]{3,2,1,0:T(8,128)(2,1)S(1)} %get-tuple-element.31), channel_id=1, source_target_pairs={{0,4},{1,5},{2,6},{3,7},{8,12},{9,13},{10,14},{11,15},{16,20},{17,... | collective-permute-start | bytes 1572872 | tf_op jit(solution)/shard_map/ppermute | solution.py:19
  70.4 9.5 %fusion.10 = (bf16[1,1,3,512,512]{4,3,2,1,0:T(8,128)(2,1)}, bf16[1,1,3,512,512]{4,3,2,1,0:T(8,128)(2,1)}, bf16[1,1,3,512,512]{4,3,2,1,0:T(8,128)(2,1)}, bf16[1,1...) fusion(bf16[3,3,3,512,512]{4,3,2,1,0:T(8,128)(2,1)} %param.12), kind=kLoop, calls=%fused_computation.53 | loop fusion | bytes 28311552 | tf_op jit(solution)/shard_map/slice | solution.py:91
  81.8 3.8 %multiply_convert_fusion = bf16[4,10,128,512]{3,2,1,0:T(8,128)(2,1)S(1)} fusion(bf16[4,1,128,512]{3,2,1,0:T(8,128)(2,1)S(1)} %get-tuple-element.30, bf16[4,8,128,512]{3,2,1,0:T(8,128)(2,1)S(1)} %constant_dynamic-update-slice_fusion, bf16[4,1,128,512]{3,2,1,0:T(8,128)(2,1)S(1)} %get-tuple-element.29, f32[512]{0:T(512)S(1)} %copy-done.29, ...), kind=kLoop, calls=%fused_computation.3 | loop fusion | flops 31457280 | bytes 10506240 | tf_op jit(solution)/shard_map/convert_element_type | solution.py:51
  85.8 5.6 %pad_maximum_fusion.9 = bf16[4,10,130,512]{3,2,1,0:T(8,128)(2,1)} fusion(bf16[4,10,1,512]{3,2,1,0:T(2,128)(2,1)S(1)} %get-tuple-element.28, bf16[4,10,128,512]{3,2,1,0:T(8,128)(2,1)S(1)} %multiply_convert_fusion, bf16[4,10,1,512]{3,2,1,0:T(2,128)(2,1)S(1)} %get-tuple-element.27), kind=kLoop, calls=%fused_computation.16 | loop fusion | flops 15974400 | bytes 10649600 | tf_op jit(solution)/shard_map/jit(_pad)/concatenate | solution.py:132
  91.3 3.3 %gather_fusion.2 = bf16[2,10,130,512]{3,2,1,0:T(8,128)(2,1)S(1)} fusion(bf16[4,10,130,512]{3,2,1,0:T(8,128)(2,1)} %pad_maximum_fusion.9, s32[1024]{0:T(1024)S(1)} %pad_clamp_fusion), kind=kCustom, calls=%fused_computation.2.clone | custom fusion | bytes 5324808 | tf_op jit(solution)/shard_map/jit(_take)/gather | solution.py:82
  94.7 4.9 %gather_fusion.1 = bf16[2,10,130,512]{3,2,1,0:T(8,128)(2,1)} fusion(bf16[4,10,130,512]{3,2,1,0:T(8,128)(2,1)} %pad_maximum_fusion.9, s32[1024]{0:T(1024)S(1)} %pad_clamp_fusion.1), kind=kCustom, calls=%fused_computation.1.clone | custom fusion | bytes 5324808 | tf_op jit(solution)/shard_map/jit(_take)/gather | solution.py:82
  99.5 4.9 %gather_fusion = bf16[2,10,130,512]{3,2,1,0:T(8,128)(2,1)} fusion(bf16[4,10,130,512]{3,2,1,0:T(8,128)(2,1)} %pad_maximum_fusion.9, s32[1024]{0:T(1024)S(1)} %pad_clamp_fusion.2), kind=kCustom, calls=%fused_computation.clone | custom fusion | bytes 5324808 | tf_op jit(solution)/shard_map/jit(_take)/gather | solution.py:82
  104.4 2.3 %broadcast_select_fusion = (bf16[2,10,130,512]{3,2,1,0:T(8,128)(2,1)S(1)}, bf16[2,10,130,512]{3,2,1,0:T(8,128)(2,1)S(1)}) fusion(bf16[2,10,130,512]{3,2,1,0:T(8,128)(2,1)S(1)} %gather_fusion.2, pred[2]{0:T(512)(128)(4,1)S(1)} %get-tuple-element.60, bf16[2,10,130,512]{3,2,1,0:T(8,128)(2,1)} %gather_fusion.1, pred[2]{0:T(512)(128)(4,1)S(1)} %get-tuple-element.62), kind=kLoop, calls=%fused_computation.21 | loop fusion | flops 2662400 | bytes 10649604 | tf_op jit(solution)/shard_map/jit(_take)/select_n | solution.py:82
  106.8 8.0 %fusion.13 = (bf16[2,8,128,512]{3,2,1,0:T(8,128)(2,1)}, bf16[2,8,128,512]{3,2,1,0:T(8,128)(2,1)}, bf16[2,8,128,512]{3,2,1,0:T(8,128)(2,1)}, bf16[2,8,128,512]{3,...) fusion(bf16[2,10,130,512]{3,2,1,0:T(8,128)(2,1)S(1)} %get-tuple, ...), kind=kLoop, calls=%fused_computation.56 | loop fusion | bytes 37748736 | tf_op jit(solution)/shard_map/slice | solution.py:86
  115.1 6.8 %fusion.14 = (bf16[2,8,128,512]{3,2,1,0:T(8,128)(2,1)S(1)}, bf16[2,8,128,512]{3,2,1,0:T(8,128)(2,1)}, bf16[2,8,128,512]{3,2,1,0:T(8,128)(2,1)}, bf16[2,8,128,512...) fusion(bf16[2,10,130,512]{3,2,1,0:T(8,128)(2,1)S(1)} %broadcast, ...), kind=kLoop, calls=%fused_computation.57 | loop fusion | bytes 37748736 | tf_op jit(solution)/shard_map/slice | solution.py:86
  121.9 7.3 %fusion.15 = (bf16[2,8,128,512]{3,2,1,0:T(8,128)(2,1)}, bf16[2,8,128,512]{3,2,1,0:T(8,128)(2,1)}, bf16[2,8,128,512]{3,2,1,0:T(8,128)(2,1)}, bf16[2,8,128,512]{3,...) fusion(bf16[2,10,130,512]{3,2,1,0:T(8,128)(2,1)S(1)} %get-tuple, ...), kind=kLoop, calls=%fused_computation.58 | loop fusion | bytes 37748736 | tf_op jit(solution)/shard_map/slice | solution.py:86
  129.2 3.7 %pad_maximum_fusion.7 = bf16[2,8,128,1536]{3,2,1,0:T(8,128)(2,1)S(1)} fusion(bf16[2,8,128,512]{3,2,1,0:T(8,128)(2,1)} %get-tuple-element.36, bf16[2,8,128,512]{3,2,1,0:T(8,128)(2,1)} %get-tuple-element.37, bf16[2,8,128,512]{3,2,1,0:T(8,128)(2,1)} %get-tuple-element.38), kind=kLoop, calls=%fused_computation.11 | loop fusion | flops 18874368 | bytes 12582912 | tf_op jit(solution)/shard_map/concatenate | solution.py:84
  132.9 4.9 %fusion.25 = f32[2048,512]{1,0:T(8,128)} fusion(bf16[2048,1536]{1,0:T(8,128)(2,1)S(1)} %bitcast.47, bf16[1536,512]{1,0:T(8,128)(2,1)S(1)} %bitcast.62), kind=kOutput, calls=%fused_computation.68 | convolution fusion | flops 3221225472 | bytes 12058624 | tf_op jit(solution)/shard_map/dot_general | solution.py:92
  137.8 4.2 %pad_maximum_fusion.6 = bf16[2,8,128,1536]{3,2,1,0:T(8,128)(2,1)S(1)} fusion(bf16[2,8,128,512]{3,2,1,0:T(8,128)(2,1)S(1)} %copy-done.18, bf16[2,8,128,512]{3,2,1,0:T(8,128)(2,1)S(1)} %copy-done.19, bf16[2,8,128,512]{3,2,1,0:T(8,128)(2,1)S(1)} %copy-done.20), kind=kLoop, calls=%fused_computation.10 | loop fusion | flops 18874368 | bytes 12582912 | tf_op jit(solution)/shard_map/concatenate | solution.py:84
  142.1 4.9 %fusion.24 = f32[2048,512]{1,0:T(8,128)} fusion(bf16[2048,1536]{1,0:T(8,128)(2,1)S(1)} %bitcast.48, bf16[1536,512]{1,0:T(8,128)(2,1)S(1)} %bitcast.61), kind=kOutput, calls=%fused_computation.67 | convolution fusion | flops 3221225472 | bytes 12058624 | tf_op jit(solution)/shard_map/dot_general | solution.py:92
  148.4 4.9 %fusion.18 = f32[2048,512]{1,0:T(8,128)} fusion(bf16[2048,1536]{1,0:T(8,128)(2,1)S(1)} %bitcast.54, bf16[1536,512]{1,0:T(8,128)(2,1)S(1)} %bitcast.60), kind=kOutput, calls=%fused_computation.61 | convolution fusion | flops 3221225472 | bytes 12058624 | tf_op jit(solution)/shard_map/dot_general | solution.py:92
  153.3 4.9 %fusion.19 = f32[2048,512]{1,0:T(8,128)} fusion(bf16[2048,1536]{1,0:T(8,128)(2,1)S(1)} %bitcast.53, bf16[1536,512]{1,0:T(8,128)(2,1)S(1)} %bitcast.59), kind=kOutput, calls=%fused_computation.62 | convolution fusion | flops 3221225472 | bytes 12058624 | tf_op jit(solution)/shard_map/dot_general | solution.py:92
  158.3 4.2 %pad_maximum_fusion.2 = bf16[2,8,128,1536]{3,2,1,0:T(8,128)(2,1)S(1)} fusion(bf16[2,8,128,512]{3,2,1,0:T(8,128)(2,1)S(1)} %copy-done.15, bf16[2,8,128,512]{3,2,1,0:T(8,128)(2,1)S(1)} %copy-done.16, bf16[2,8,128,512]{3,2,1,0:T(8,128)(2,1)S(1)} %copy-done.17), kind=kLoop, calls=%fused_computation.6 | loop fusion | flops 18874368 | bytes 12582912 | tf_op jit(solution)/shard_map/concatenate | solution.py:84
  162.6 4.9 %fusion.20 = f32[2048,512]{1,0:T(8,128)} fusion(bf16[2048,1536]{1,0:T(8,128)(2,1)S(1)} %bitcast.49, bf16[1536,512]{1,0:T(8,128)(2,1)S(1)} %bitcast.58), kind=kOutput, calls=%fused_computation.63 | convolution fusion | flops 3221225472 | bytes 12058624 | tf_op jit(solution)/shard_map/dot_general | solution.py:92
  167.5 4.2 %pad_maximum_fusion.3 = bf16[2,8,128,1536]{3,2,1,0:T(8,128)(2,1)S(1)} fusion(bf16[2,8,128,512]{3,2,1,0:T(8,128)(2,1)S(1)} %copy-done.13, bf16[2,8,128,512]{3,2,1,0:T(8,128)(2,1)S(1)} %copy-done.14, bf16[2,8,128,512]{3,2,1,0:T(8,128)(2,1)S(1)} %copy-done.12), kind=kLoop, calls=%fused_computation.7 | loop fusion | flops 18874368 | bytes 12582912 | tf_op jit(solution)/shard_map/concatenate | solution.py:84
  171.7 5.0 %fusion.21 = f32[2048,512]{1,0:T(8,128)} fusion(bf16[2048,1536]{1,0:T(8,128)(2,1)S(1)} %bitcast.50, bf16[1536,512]{1,0:T(8,128)(2,1)S(1)} %bitcast.57), kind=kOutput, calls=%fused_computation.64 | convolution fusion | flops 3221225472 | bytes 12058624 | tf_op jit(solution)/shard_map/dot_general | solution.py:92
  176.7 4.5 %pad_maximum_fusion.5 = bf16[2,8,128,1536]{3,2,1,0:T(8,128)(2,1)S(1)} fusion(bf16[2,8,128,512]{3,2,1,0:T(8,128)(2,1)S(1)} %copy-done.9, bf16[2,8,128,512]{3,2,1,0:T(8,128)(2,1)S(1)} %copy-done.10, bf16[2,8,128,512]{3,2,1,0:T(8,128)(2,1)S(1)} %copy-done.11), kind=kLoop, calls=%fused_computation.9 | loop fusion | flops 18874368 | bytes 12582912 | tf_op jit(solution)/shard_map/concatenate | solution.py:84
  181.2 4.9 %fusion.23 = f32[2048,512]{1,0:T(8,128)} fusion(bf16[2048,1536]{1,0:T(8,128)(2,1)S(1)} %bitcast.51, bf16[1536,512]{1,0:T(8,128)(2,1)S(1)} %bitcast.56), kind=kOutput, calls=%fused_computation.66 | convolution fusion | flops 3221225472 | bytes 12058624 | tf_op jit(solution)/shard_map/dot_general | solution.py:92
  186.2 4.2 %pad_maximum_fusion.4 = bf16[2,8,128,1536]{3,2,1,0:T(8,128)(2,1)S(1)} fusion(bf16[2,8,128,512]{3,2,1,0:T(8,128)(2,1)S(1)} %get-tuple-element.55, bf16[2,8,128,512]{3,2,1,0:T(8,128)(2,1)S(1)} %copy-done.7, bf16[2,8,128,512]{3,2,1,0:T(8,128)(2,1)S(1)} %copy-done.8), kind=kLoop, calls=%fused_computation.8 | loop fusion | flops 18874368 | bytes 12582912 | tf_op jit(solution)/shard_map/concatenate | solution.py:84
  190.4 4.9 %fusion.22 = f32[2048,512]{1,0:T(8,128)} fusion(bf16[2048,1536]{1,0:T(8,128)(2,1)S(1)} %bitcast.52, bf16[1536,512]{1,0:T(8,128)(2,1)S(1)} %bitcast.55), kind=kOutput, calls=%fused_computation.65 | convolution fusion | flops 3221225472 | bytes 12058624 | tf_op jit(solution)/shard_map/dot_general | solution.py:92
  195.4 4.2 %pad_maximum_fusion.8 = bf16[2,8,128,1536]{3,2,1,0:T(8,128)(2,1)S(1)} fusion(bf16[2,8,128,512]{3,2,1,0:T(8,128)(2,1)S(1)} %copy-done.5, bf16[2,8,128,512]{3,2,1,0:T(8,128)(2,1)S(1)} %copy-done.6, bf16[2,8,128,512]{3,2,1,0:T(8,128)(2,1)S(1)} %copy-done.4), kind=kLoop, calls=%fused_computation.12 | loop fusion | flops 18874368 | bytes 12582912 | tf_op jit(solution)/shard_map/concatenate | solution.py:84
  199.6 14.8 %add_add_fusion = f32[2048,512]{1,0:T(8,128)} fusion(f32[2048,512]{1,0:T(8,128)} %fusion.25, f32[2048,512]{1,0:T(8,128)} %fusion.24, f32[2048,512]{1,0:T(8,128)} %fusion.23, f32[2048,512]{1,0:T(8,128)} %fusion.22, f32[2048,512]{1,0:T(8,128)} %fusion.21, f32[2048,512]{1,0:T(8,128)} %fusion.20, f32[2048,512]{1,0:T(8,128)} %fusion.18, ...), kind=kOutput, calls=%fused_computation.20 | convolution fusion | flops 3229614080 | bytes 45613056 | tf_op jit(solution)/shard_map/dot_general | solution.py:92
  214.5 4.4 %fusion.2 = bf16[2,8,128,512]{3,2,1,0:T(8,128)(2,1)} fusion(f32[2,8,128,512]{3,2,1,0:T(8,128)} %bitcast.45, bf16[2,8,128,512]{3,2,1,0:T(8,128)(2,1)S(1)} %copy-done.1, f32[512]{0:T(512)S(1)} %copy-done.31), kind=kLoop, calls=%fused_computation.19 | loop fusion | flops 4194304 | bytes 8390656 | tf_op jit(solution)/shard_map/convert_element_type | solution.py:142
  (95 shorter events, 8.8 us)
Async XLA Ops:
  0.0 65.4 %copy-start = (bf16[2,8,128,512]{3,2,1,0:T(8,128)(2,1)S(1)}, bf16[2,8,128,512]{3,2,1,0:T(8,128)(2,1)}, u32[]{:S(2)}) copy-start(bf16[2,8,128,512]{3,2,1,0:T(8,128)(2,1)} %param.8) | copy-start | bytes 6291460
  0.0 63.6 %collective-permute-start = (bf16[2,8,128,512]{3,2,1,0:T(8,128)(2,1)}, bf16[2,8,128,512]{3,2,1,0:T(8,128)(2,1)}, u32[]{:S(2)}, u32[]{:S(2)}) collective-permute-start(bf16[2,8,128,512]{3,2,1,0:T(8,128)(2,1)} %param.8), channel_id=1, source_target_pairs={{0,1},{1,2},{2,3},{3,8},{8,9},{9,10},{10,11},{11,16},{16,17},{17,1... | collective-permute-start | bytes 6291464 | tf_op jit(solution)/shard_map/ppermute | solution.py:28
  65.7 14.2 %collective-permute-start.1 = (bf16[4,1,128,512]{3,2,1,0:T(8,128)(2,1)S(1)}, bf16[4,1,128,512]{3,2,1,0:T(8,128)(2,1)S(1)}, u32[]{:S(2)}, u32[]{:S(2)}) collective-permute-start(bf16[4,1,128,512]{3,2,1,0:T(8,128)(2,1)S(1)} %get-tuple-element.31), channel_id=1, source_target_pairs={{0,4},{1,5},{2,6},{3,7},{8,12},{9,13},{10,14},{11,15},{16,20},{17,... | collective-permute-start | bytes 1572872 | tf_op jit(solution)/shard_map/ppermute | solution.py:19
  68.9 12.9 %copy-start.29 = (f32[512]{0:T(512)S(1)}, f32[512]{0:T(512)}, u32[]{:S(2)}) copy-start(f32[512]{0:T(512)} %param.11) | copy-start | bytes 6148
  68.9 12.9 %copy-start.30 = (f32[512]{0:T(512)S(1)}, f32[512]{0:T(512)}, u32[]{:S(2)}) copy-start(f32[512]{0:T(512)} %param.10) | copy-start | bytes 6148
  68.9 12.8 %collective-permute-start.2 = (bf16[4,1,128,512]{3,2,1,0:T(8,128)(2,1)S(1)}, bf16[4,1,128,512]{3,2,1,0:T(8,128)(2,1)S(1)}, u32[]{:S(2)}, u32[]{:S(2)}) collective-permute-start(bf16[4,1,128,512]{3,2,1,0:T(8,128)(2,1)S(1)} %get-tuple-element.32), channel_id=1, source_target_pairs={{4,0},{5,1},{6,2},{7,3},{12,8},{13,9},{14,10},{15,11},{20,16},{21,... | collective-permute-start | bytes 1572872 | tf_op jit(solution)/shard_map/ppermute | solution.py:20
  106.8 8.0 %copy-start.2 = (bf16[2,10,130,512]{3,2,1,0:T(8,128)(2,1)S(1)}, bf16[2,10,130,512]{3,2,1,0:T(8,128)(2,1)}, u32[]{:S(2)}) copy-start(bf16[2,10,130,512]{3,2,1,0:T(8,128)(2,1)} %gather_fusion) | copy-start | bytes 7987204
  132.9 5.0 %copy-start.18 = (bf16[2,8,128,512]{3,2,1,0:T(8,128)(2,1)S(1)}, bf16[2,8,128,512]{3,2,1,0:T(8,128)(2,1)}, u32[]{:S(2)}) copy-start(bf16[2,8,128,512]{3,2,1,0:T(8,128)(2,1)} %get-tuple-element.39) | copy-start | bytes 6291460
  132.9 5.0 %copy-start.19 = (bf16[2,8,128,512]{3,2,1,0:T(8,128)(2,1)S(1)}, bf16[2,8,128,512]{3,2,1,0:T(8,128)(2,1)}, u32[]{:S(2)}) copy-start(bf16[2,8,128,512]{3,2,1,0:T(8,128)(2,1)} %get-tuple-element.40) | copy-start | bytes 6291460
  132.9 4.9 %copy-start.20 = (bf16[2,8,128,512]{3,2,1,0:T(8,128)(2,1)S(1)}, bf16[2,8,128,512]{3,2,1,0:T(8,128)(2,1)}, u32[]{:S(2)}) copy-start(bf16[2,8,128,512]{3,2,1,0:T(8,128)(2,1)} %get-tuple-element.41) | copy-start | bytes 6291460
  137.8 4.2 %copy-start.27 = (bf16[1,1,3,512,512]{4,3,2,1,0:T(8,128)(2,1)S(1)}, bf16[1,1,3,512,512]{4,3,2,1,0:T(8,128)(2,1)}, u32[]{:S(2)}) copy-start(bf16[1,1,3,512,512]{4,3,2,1,0:T(8,128)(2,1)} %get-tuple-element.19) | copy-start | bytes 4718596
  142.1 5.0 %copy-start.3 = (bf16[2,8,128,512]{3,2,1,0:T(8,128)(2,1)S(1)}, bf16[2,8,128,512]{3,2,1,0:T(8,128)(2,1)}, u32[]{:S(2)}) copy-start(bf16[2,8,128,512]{3,2,1,0:T(8,128)(2,1)} %get-tuple-element.50) | copy-start | bytes 6291460
  148.4 4.9 %copy-start.25 = (bf16[1,1,3,512,512]{4,3,2,1,0:T(8,128)(2,1)S(1)}, bf16[1,1,3,512,512]{4,3,2,1,0:T(8,128)(2,1)}, u32[]{:S(2)}) copy-start(bf16[1,1,3,512,512]{4,3,2,1,0:T(8,128)(2,1)} %get-tuple-element.24) | copy-start | bytes 4718596
  153.3 4.9 %copy-start.15 = (bf16[2,8,128,512]{3,2,1,0:T(8,128)(2,1)S(1)}, bf16[2,8,128,512]{3,2,1,0:T(8,128)(2,1)}, u32[]{:S(2)}) copy-start(bf16[2,8,128,512]{3,2,1,0:T(8,128)(2,1)} %get-tuple-element.43) | copy-start | bytes 6291460
  153.3 4.9 %copy-start.16 = (bf16[2,8,128,512]{3,2,1,0:T(8,128)(2,1)S(1)}, bf16[2,8,128,512]{3,2,1,0:T(8,128)(2,1)}, u32[]{:S(2)}) copy-start(bf16[2,8,128,512]{3,2,1,0:T(8,128)(2,1)} %get-tuple-element.44) | copy-start | bytes 6291460
  153.3 4.9 %copy-start.17 = (bf16[2,8,128,512]{3,2,1,0:T(8,128)(2,1)S(1)}, bf16[2,8,128,512]{3,2,1,0:T(8,128)(2,1)}, u32[]{:S(2)}) copy-start(bf16[2,8,128,512]{3,2,1,0:T(8,128)(2,1)} %get-tuple-element.45) | copy-start | bytes 6291460
  158.3 4.2 %copy-start.24 = (bf16[1,1,3,512,512]{4,3,2,1,0:T(8,128)(2,1)S(1)}, bf16[1,1,3,512,512]{4,3,2,1,0:T(8,128)(2,1)}, u32[]{:S(2)}) copy-start(bf16[1,1,3,512,512]{4,3,2,1,0:T(8,128)(2,1)} %get-tuple-element.23) | copy-start | bytes 4718596
  162.5 4.9 %copy-start.12 = (bf16[2,8,128,512]{3,2,1,0:T(8,128)(2,1)S(1)}, bf16[2,8,128,512]{3,2,1,0:T(8,128)(2,1)}, u32[]{:S(2)}) copy-start(bf16[2,8,128,512]{3,2,1,0:T(8,128)(2,1)} %get-tuple-element.51) | copy-start | bytes 6291460
  162.5 4.9 %copy-start.13 = (bf16[2,8,128,512]{3,2,1,0:T(8,128)(2,1)S(1)}, bf16[2,8,128,512]{3,2,1,0:T(8,128)(2,1)}, u32[]{:S(2)}) copy-start(bf16[2,8,128,512]{3,2,1,0:T(8,128)(2,1)} %get-tuple-element.58) | copy-start | bytes 6291460
  162.5 4.9 %copy-start.14 = (bf16[2,8,128,512]{3,2,1,0:T(8,128)(2,1)S(1)}, bf16[2,8,128,512]{3,2,1,0:T(8,128)(2,1)}, u32[]{:S(2)}) copy-start(bf16[2,8,128,512]{3,2,1,0:T(8,128)(2,1)} %get-tuple-element.59) | copy-start | bytes 6291460
  167.5 4.2 %copy-start.23 = (bf16[1,1,3,512,512]{4,3,2,1,0:T(8,128)(2,1)S(1)}, bf16[1,1,3,512,512]{4,3,2,1,0:T(8,128)(2,1)}, u32[]{:S(2)}) copy-start(bf16[1,1,3,512,512]{4,3,2,1,0:T(8,128)(2,1)} %get-tuple-element.22) | copy-start | bytes 4718596
  171.7 5.0 %copy-start.9 = (bf16[2,8,128,512]{3,2,1,0:T(8,128)(2,1)S(1)}, bf16[2,8,128,512]{3,2,1,0:T(8,128)(2,1)}, u32[]{:S(2)}) copy-start(bf16[2,8,128,512]{3,2,1,0:T(8,128)(2,1)} %get-tuple-element.52) | copy-start | bytes 6291460
  171.7 5.0 %copy-start.10 = (bf16[2,8,128,512]{3,2,1,0:T(8,128)(2,1)S(1)}, bf16[2,8,128,512]{3,2,1,0:T(8,128)(2,1)}, u32[]{:S(2)}) copy-start(bf16[2,8,128,512]{3,2,1,0:T(8,128)(2,1)} %get-tuple-element.53) | copy-start | bytes 6291460
  171.7 5.0 %copy-start.11 = (bf16[2,8,128,512]{3,2,1,0:T(8,128)(2,1)S(1)}, bf16[2,8,128,512]{3,2,1,0:T(8,128)(2,1)}, u32[]{:S(2)}) copy-start(bf16[2,8,128,512]{3,2,1,0:T(8,128)(2,1)} %get-tuple-element.54) | copy-start | bytes 6291460
  176.7 4.5 %copy-start.22 = (bf16[1,1,3,512,512]{4,3,2,1,0:T(8,128)(2,1)S(1)}, bf16[1,1,3,512,512]{4,3,2,1,0:T(8,128)(2,1)}, u32[]{:S(2)}) copy-start(bf16[1,1,3,512,512]{4,3,2,1,0:T(8,128)(2,1)} %get-tuple-element.20) | copy-start | bytes 4718596
  181.2 4.9 %copy-start.7 = (bf16[2,8,128,512]{3,2,1,0:T(8,128)(2,1)S(1)}, bf16[2,8,128,512]{3,2,1,0:T(8,128)(2,1)}, u32[]{:S(2)}) copy-start(bf16[2,8,128,512]{3,2,1,0:T(8,128)(2,1)} %get-tuple-element.56) | copy-start | bytes 6291460
  181.2 4.9 %copy-start.8 = (bf16[2,8,128,512]{3,2,1,0:T(8,128)(2,1)S(1)}, bf16[2,8,128,512]{3,2,1,0:T(8,128)(2,1)}, u32[]{:S(2)}) copy-start(bf16[2,8,128,512]{3,2,1,0:T(8,128)(2,1)} %get-tuple-element.57) | copy-start | bytes 6291460
  190.4 5.0 %copy-start.4 = (bf16[2,8,128,512]{3,2,1,0:T(8,128)(2,1)S(1)}, bf16[2,8,128,512]{3,2,1,0:T(8,128)(2,1)}, u32[]{:S(2)}) copy-start(bf16[2,8,128,512]{3,2,1,0:T(8,128)(2,1)} %get-tuple-element.33) | copy-start | bytes 6291460
  190.4 4.9 %copy-start.5 = (bf16[2,8,128,512]{3,2,1,0:T(8,128)(2,1)S(1)}, bf16[2,8,128,512]{3,2,1,0:T(8,128)(2,1)}, u32[]{:S(2)}) copy-start(bf16[2,8,128,512]{3,2,1,0:T(8,128)(2,1)} %get-tuple-element.34) | copy-start | bytes 6291460
  190.4 4.9 %copy-start.6 = (bf16[2,8,128,512]{3,2,1,0:T(8,128)(2,1)S(1)}, bf16[2,8,128,512]{3,2,1,0:T(8,128)(2,1)}, u32[]{:S(2)}) copy-start(bf16[2,8,128,512]{3,2,1,0:T(8,128)(2,1)} %get-tuple-element.35) | copy-start | bytes 6291460
  199.6 14.8 %copy-start.1 = (bf16[2,8,128,512]{3,2,1,0:T(8,128)(2,1)S(1)}, bf16[2,8,128,512]{3,2,1,0:T(8,128)(2,1)}, u32[]{:S(2)}) copy-start(bf16[2,8,128,512]{3,2,1,0:T(8,128)(2,1)} %param.8) | copy-start | bytes 6291460
  199.6 14.8 %copy-start.31 = (f32[512]{0:T(512)S(1)}, f32[512]{0:T(512)}, u32[]{:S(2)}) copy-start(f32[512]{0:T(512)} %param.13) | copy-start | bytes 6148
  (3 other events, 9.3 us)
where the time goes:
time: 223 us; the launch traced here: 219 us
  matrix products  54.9 us (25%)
  blocking collectives  53.6 us (24%)
  other arithmetic  51.1 us (23%)
  local copies, waits for them, and re-layouts  47.8 us (21%)
  starting transfers between devices  9.25 us (4%)
    dot_general x9, matrix products, convolve(): jnp.dot(stacked.reshape(frame_count * row_count * col_count, 3 * channels...  54.2 us
    psum x1, blocking collectives, finish_stats(): lax.psum((local_sums, local_squares), ('req', 'tile', 'span'))  53.6 us
    concatenate x8, other arithmetic, convolve(): jnp.concatenate([chosen[:, row_tap:row_tap + row_count, col_tap:col_tap +...  30.4 us
    slice x3, local copies, waits for them, and re-layouts, convolve(): chosen[:, row_tap:row_tap + row_count, col_tap:col_tap + col_count]  22.1 us
    gather x3, local copies, waits for them, and re-layouts, convolve(): chosen = jnp.take(padded, tap_index[time_tap], axis=0)  13.1 us
    slice x1, local copies, waits for them, and re-layouts, convolve(): kernel = conv_weight[time_tap, row_tap].reshape(3 * channels, channels)  9.52 us
    concatenate x1, other arithmetic, shards(): padded = jnp.pad(extended, ((0, 0), (0, 0), (1, 1), (0, 0)), mode='edge')  5.56 us
    ppermute x1, starting transfers between devices, shifted(): return lax.ppermute(array, axis, pairs)  4.63 us
  transfers between devices with their start and end apart: 3, of which 1 were waited for; matrix products, arithmetic and copies ran while one was open for 7% of the time, Pallas kernels for 0%

commit v1 on v0

v1 whole, which is shorter than its diff:
```python
import functools

import jax
import jax.numpy as jnp
from jax import lax
from jax.experimental import pallas as pl
from jax.experimental.pallas import tpu as pltpu
from jax.sharding import PartitionSpec as P

GROUPS = 32
EPSILON = 1e-06
MESH = pl.DeviceIdType.MESH
HIGHEST = lax.Precision.HIGHEST
F32 = jnp.float32


def kernel(
    sizes,
    counts,
    lat,
    gain,
    shift,
    bias,
    weight,
    out,
    own,
    prev,
    rim,
    wv,
    hid,
    acc,
    msg,
    stat_a,
    stat_b,
    table,
    own_sem,
    w_sem,
    out_sem,
    a_send,
    a_recv,
    b_send,
    b_recv,
    rim_send,
    rim_recv,
    frame_send,
    frame_recv,
):
    reqs_n, tiles, spans = sizes
    frames, rows, cols, channels = own.shape
    per_group = channels // GROUPS
    requests = counts.shape[0]
    req, tile, span = (lax.axis_index("req"), lax.axis_index("tile"), lax.axis_index("span"))
    place = req * spans + span
    places = reqs_n * spans
    has_next, has_prev = place < places - 1, place > 0
    has_up, has_down = tile > 0, tile < tiles - 1

    def at(chain, row):
        return {"req": chain // spans, "tile": row, "span": chain % spans}

    def chain_to(by):
        return jnp.clip(place + by, 0, places - 1)

    members_a = tiles * spans
    me_a = tile * spans + span

    def partner_a(k):
        other = (me_a + k) % members_a
        return {"req": req, "tile": other // spans, "span": other % spans}

    def partner_b(k):
        return {"req": (req + k) % reqs_n, "tile": tile, "span": span}

    for f in range(frames):
        pltpu.make_async_copy(lat.at[f], own.at[f], own_sem.at[f]).start()

    barrier = pltpu.get_barrier_semaphore()
    for k in range(1, members_a):
        pl.semaphore_signal(barrier, inc=1, device_id=partner_a(k), device_id_type=MESH)
    for k in range(1, reqs_n):
        pl.semaphore_signal(barrier, inc=1, device_id=partner_b(k), device_id_type=MESH)
    for by, has in ((1, has_next), (-1, has_prev)):

        @pl.when(has)
        def _():
            pl.semaphore_signal(
                barrier, inc=1, device_id=at(chain_to(by), tile), device_id_type=MESH
            )

        for step, has_row in ((-1, has_up), (1, has_down)):

            @pl.when(has & has_row)
            def _():
                pl.semaphore_signal(
                    barrier,
                    inc=1,
                    device_id=at(chain_to(by), jnp.clip(tile + step, 0, tiles - 1)),
                    device_id_type=MESH,
                )

    for t in (2, 1, 0):
        for b in range(3):
            i = 3 * t + b
            pltpu.make_async_copy(weight.at[i], wv.at[i], w_sem.at[i]).start()

    start_of, end_of, total = [], [], jnp.int32(0)
    for r in range(requests):
        start_of.append(total)
        total = total + counts[r]
        end_of.append(total)
    first = place * frames

    def member(slot, r):
        position = first + slot - 2
        return (position >= start_of[r]) & (position < end_of[r])

    def start_at(slot):
        found = jnp.int32(0)
        for r in range(requests):
            found = jnp.where(member(slot, r), start_of[r], found)
        return found

    per_frame = []
    for f in range(frames):
        pltpu.make_async_copy(lat.at[f], own.at[f], own_sem.at[f]).wait()

        def add_row(i, carry):
            s, q = carry
            x = own[f, i].astype(F32).reshape(cols // 8, 8, channels)
            return (s + jnp.sum(x, axis=0), q + jnp.sum(x * x, axis=0))

        zero = jnp.zeros((8, channels), F32)
        s, q = lax.fori_loop(0, rows, add_row, (zero, zero))
        per_frame.append((jnp.sum(s, axis=0, keepdims=True), jnp.sum(q, axis=0, keepdims=True)))
    table[...] = jnp.zeros_like(table)
    for r in range(requests):
        for which in range(2):
            line = jnp.zeros((1, channels), F32)
            for f in range(frames):
                line = line + jnp.where(member(f + 2, r), per_frame[f][which], 0.0)
            table[which * requests + r : which * requests + r + 1, :] = line
    lanes = msg.shape[1]
    to_group = (
        lax.broadcasted_iota(jnp.int32, (channels, lanes), 0) // per_group
        == lax.broadcasted_iota(jnp.int32, (channels, lanes), 1)
    ).astype(F32)
    from_group = (
        lax.broadcasted_iota(jnp.int32, (lanes, channels), 1) // per_group
        == lax.broadcasted_iota(jnp.int32, (lanes, channels), 0)
    ).astype(F32)
    msg[...] = jnp.dot(table[...], to_group, precision=HIGHEST, preferred_element_type=F32)
    stat_a[me_a] = msg[...]

    near = has_up.astype(jnp.int32) + has_down.astype(jnp.int32)
    sides = has_next.astype(jnp.int32) + has_prev.astype(jnp.int32)
    pl.semaphore_wait(barrier, members_a - 1 + reqs_n - 1 + sides * (1 + near))

    def copy_a(k):
        return pltpu.make_async_remote_copy(
            src_ref=msg,
            dst_ref=stat_a.at[me_a],
            send_sem=a_send.at[k],
            recv_sem=a_recv.at[me_a],
            device_id=partner_a(k),
            device_id_type=MESH,
        )

    def copy_b(k):
        return pltpu.make_async_remote_copy(
            src_ref=table.at[:, 0:lanes],
            dst_ref=stat_b.at[req],
            send_sem=b_send.at[k],
            recv_sem=b_recv.at[req],
            device_id=partner_b(k),
            device_id_type=MESH,
        )

    def rim_copy(slot, side):
        edge = rows - 1 if side == 0 else 0
        row_to = jnp.clip(tile + (1 if side == 0 else -1), 0, tiles - 1)
        forward = slot == 0
        source = lat.at[frames - 2 : frames, edge] if forward else lat.at[:, edge]
        count = 2 if forward else frames
        return pltpu.make_async_remote_copy(
            src_ref=source,
            dst_ref=rim.at[side, slot : slot + count],
            send_sem=rim_send.at[side, slot // 2],
            recv_sem=rim_recv.at[side, slot // 2],
            device_id=at(chain_to(1) if forward else place, row_to),
            device_id_type=MESH,
        )

    def frame_copy(slot):
        return pltpu.make_async_remote_copy(
            src_ref=lat.at[frames - 2 + slot],
            dst_ref=prev.at[slot],
            send_sem=frame_send.at[slot],
            recv_sem=frame_recv.at[slot],
            device_id=at(chain_to(1), tile),
            device_id_type=MESH,
        )

    row_sends = ((0, has_down), (1, has_up))
    row_recvs = ((0, has_up), (1, has_down))

    for k in range(1, members_a):
        copy_a(k).start()
    for side, has in row_sends:
        pl.when(has)(lambda side=side: rim_copy(2, side).start())
    pl.when(has_next)(lambda: frame_copy(1).start())

    for k in range(1, members_a):
        copy_a(k).wait_send()
        other = (me_a + k) % members_a
        pltpu.make_async_remote_copy(
            src_ref=msg,
            dst_ref=stat_a.at[other],
            send_sem=a_send.at[k],
            recv_sem=a_recv.at[other],
            device_id=partner_a(k),
            device_id_type=MESH,
        ).wait_recv()
    part = jnp.sum(stat_a[...], axis=0)
    table[:, 0:lanes] = part
    stat_b[req] = part
    for k in range(1, reqs_n):
        copy_b(k).start()
    for side, has in row_sends:
        pl.when(has & has_next)(lambda side=side: rim_copy(0, side).start())
    pl.when(has_next)(lambda: frame_copy(0).start())
    for k in range(1, reqs_n):
        copy_b(k).wait_send()
        other = (req + k) % reqs_n
        pltpu.make_async_remote_copy(
            src_ref=table.at[:, 0:lanes],
            dst_ref=stat_b.at[other],
            send_sem=b_send.at[k],
            recv_sem=b_recv.at[other],
            device_id=partner_b(k),
            device_id_type=MESH,
        ).wait_recv()
    whole = jnp.sum(stat_b[...], axis=0)
    cells = rows * tiles * cols * per_group
    lines = []
    for r in range(requests):
        n = jnp.full((1, lanes), counts[r] * cells, jnp.int32).astype(F32)
        mean = whole[r : r + 1] / n
        scale = lax.rsqrt(whole[requests + r : requests + r + 1] / n - mean * mean + EPSILON)
        lines.append((mean, scale))
    for r in range(requests):
        msg[r : r + 1, :] = lines[r][0]
        msg[requests + r : requests + r + 1, :] = lines[r][1]
    table[...] = jnp.dot(msg[...], from_group, precision=HIGHEST, preferred_element_type=F32)

    lane = min(128, channels)
    first_col = lax.broadcasted_iota(jnp.int32, (cols, lane), 0) == 0
    last_col = lax.broadcasted_iota(jnp.int32, (cols, lane), 0) == cols - 1

    def coefficients(slot):
        mean = jnp.zeros((1, channels), F32)
        scale = jnp.zeros((1, channels), F32)
        for r in range(requests):
            inside = member(slot, r)
            mean = jnp.where(inside, table[r : r + 1, :], mean)
            scale = jnp.where(inside, table[requests + r : requests + r + 1, :], scale)
        return mean, scale * gain[...] * 0.5, shift[...] * 0.5

    def put_row(slot, row, read, coef):
        mean, factor, offset = coef
        for c in range(0, channels, lane):
            part = slice(c, c + lane)
            x = read(part).astype(F32)
            h = (x - mean[:, part]) * factor[:, part] + offset[:, part]
            y = h + h * jnp.tanh(h)
            left = jnp.where(first_col, y, pltpu.roll(y, 1, 0))
            right = jnp.where(last_col, y, pltpu.roll(y, cols - 1, 0))
            hid[slot, row, :, c : c + lane] = left.astype(jnp.bfloat16)
            hid[slot, row, :, channels + c : channels + c + lane] = y.astype(jnp.bfloat16)
            hid[slot, row, :, 2 * channels + c : 2 * channels + c + lane] = right.astype(
                jnp.bfloat16
            )

    def put_frame(slot, source, index):
        coef = coefficients(slot)

        def body(i, _):
            put_row(slot, i + 1, lambda part: source[index, i, :, part], coef)
            return 0

        lax.fori_loop(0, rows, body, 0)
        for side, has in row_recvs:
            row = 0 if side == 0 else rows + 1
            edge = 0 if side == 0 else rows - 1

            @pl.when(has)
            def _():
                put_row(slot, row, lambda part: rim[side, slot, :, part], coef)

            @pl.when(jnp.logical_not(has))
            def _():
                hid[slot, row] = hid[slot, 1 + edge]

    def multiply(f, t, begin, end):
        source = jnp.maximum(first + f - 2 + t, start_at(f + 2)) - first + 2

        def body(b, _):
            if begin:
                i = 3 * t + b
                pltpu.make_async_copy(weight.at[i], wv.at[i], w_sem.at[i]).wait()
            lhs = hid[source, pl.ds(b, rows)].reshape(rows * cols, 3 * channels)
            acc[f] += jnp.dot(lhs, wv[3 * t + b], preferred_element_type=F32)
            return 0

        lax.fori_loop(0, 3, body, 0)
        if end:
            value = own[f].reshape(rows * cols, channels).astype(F32) + acc[f] + bias[...]
            own[f] = value.astype(jnp.bfloat16).reshape(rows, cols, channels)
            pltpu.make_async_copy(own.at[f], out.at[f], out_sem.at[f]).start()

    for side, has in row_recvs:
        pl.when(has)(lambda side=side: rim_copy(2, side).wait_recv())
    for f in range(frames):
        put_frame(f + 2, own, f)
    acc[...] = jnp.zeros_like(acc)

    pairs = [(f, t) for f in range(frames) for t in (2, 1, 0)]
    order = sorted(pairs, key=lambda p: (max(0, 2 - p[0] - p[1]), -p[1], -p[0]))
    seen, left = set(), {f: 3 for f in range(frames)}
    ready = 0
    for f, t in order:
        need = max(0, 2 - f - t)
        while ready < need:
            ready += 1
            slot = 2 - ready

            @pl.when(has_prev)
            def _():
                frame_copy(slot).wait_recv()
                if ready == 1:
                    for side, has in row_recvs:
                        pl.when(has)(lambda side=side: rim_copy(0, side).wait_recv())
                put_frame(slot, prev, slot)

        left[f] -= 1
        multiply(f, t, t not in seen, left[f] == 0)
        seen.add(t)

    for side, has in row_sends:
        pl.when(has)(lambda side=side: rim_copy(2, side).wait_send())
        pl.when(has & has_next)(lambda side=side: rim_copy(0, side).wait_send())
    for slot in range(2):
        pl.when(has_next)(lambda slot=slot: frame_copy(slot).wait_send())
    for f in range(frames):
        pltpu.make_async_copy(own.at[f], out.at[f], out_sem.at[f]).wait()


def solution(mesh):
    sizes = (mesh.shape["req"], mesh.shape["tile"], mesh.shape["span"])
    reqs_n, tiles, spans = sizes

    def step(latents, frame_counts, norm_gain, norm_shift, conv_weight, conv_bias):
        frames, rows, cols, channels = latents.shape
        taps = conv_weight.shape[1] * conv_weight.shape[2]
        lines = -(-2 * frame_counts.shape[0] // 8) * 8
        members = tiles * spans
        bf16, dma = jnp.bfloat16, pltpu.SemaphoreType.DMA
        weight = conv_weight.reshape(9, 3 * channels, channels)
        whole = pl.BlockSpec(memory_space=pltpu.VMEM)
        anywhere = pl.BlockSpec(memory_space=pl.ANY)
        positions = frames * rows * cols
        return pl.pallas_call(
            functools.partial(kernel, sizes),
            out_shape=jax.ShapeDtypeStruct(latents.shape, bf16),
            in_specs=[
                pl.BlockSpec(memory_space=pltpu.SMEM),
                anywhere,
                whole,
                whole,
                whole,
                anywhere,
            ],
            out_specs=anywhere,
            scratch_shapes=[
                pltpu.VMEM((frames, rows, cols, channels), bf16),
                pltpu.VMEM((2, rows, cols, channels), bf16),
                pltpu.VMEM((2, frames + 2, cols, channels), bf16),
                pltpu.VMEM((9, 3 * channels, channels), bf16),
                pltpu.VMEM((frames + 2, rows + 2, cols, 3 * channels), bf16),
                pltpu.VMEM((frames, rows * cols, channels), F32),
                pltpu.VMEM((lines, 128), F32),
                pltpu.VMEM((members, lines, 128), F32),
                pltpu.VMEM((reqs_n, lines, 128), F32),
                pltpu.VMEM((lines, channels), F32),
                dma((frames,)),
                dma((9,)),
                dma((frames,)),
                dma((members,)),
                dma((members,)),
                dma((reqs_n,)),
                dma((reqs_n,)),
                dma((2, 2)),
                dma((2, 2)),
                dma((2,)),
                dma((2,)),
            ],
            compiler_params=pltpu.CompilerParams(
                collective_id=0, has_side_effects=True, vmem_limit_bytes=56 * 1024 * 1024
            ),
            cost_estimate=pl.CostEstimate(
                flops=2 * positions * 3 * taps * channels * channels,
                bytes_accessed=2 * 3 * taps * channels * channels + 4 * positions * channels,
                transcendentals=2 * positions * channels,
            ),
        )(
            frame_counts,
            latents,
            norm_gain.reshape(1, channels),
            norm_shift.reshape(1, channels),
            conv_bias.reshape(1, channels),
            weight,
        )

    placed = (P(("req", "span"), "tile", None, None), P(), P(), P(), P(), P())
    return jax.shard_map(
        step,
        mesh=mesh,
        in_specs=placed,
        out_specs=P(("req", "span"), "tile", None, None),
        check_vma=False,
    )
```

time: 223 us -> 60 us (0.27)
  the two profiles are of different devices: /device:TPU:1 before, /device:TPU:15 now
where the time goes in v1:
time: 60 us; the launch traced here: 59.8 us
  Pallas kernels  56.7 us (94%)
  local copies, waits for them, and re-layouts  3.1 us (5%)
    pallas_call x1, Pallas kernels, step(): pl.pallas_call(functools.partial(kernel, sizes), out_shape=jax.ShapeDtype...  56.7 us
    unnamed x1, local copies, waits for them, and re-layouts  3.1 us

profile of v1, /device:TPU:15, one launch (start us, length us, event | category | flops | bytes accessed | tf_op | source)
XLA Modules:
  0.0 59.8 jit_solution(6424096321954257433)
XLA Ops:
  0.0 56.7 %shard_map.64 = bf16[2,8,128,512]{3,2,1,0:T(8,128)(2,1)} custom-call(s32[4]{0:T(128)} %counts.1, bf16[2,8,128,512]{3,2,1,0:T(8,128)(2,1)} %lat.1, f32[1,512]{1,0:T(1,128)} %bitcast.5, f32[1,512]{1,0:T(1,128)} %bitcast.6, f32[1,512]{1,0:T(1,128)} %bitcast.7, bf16[9,1536,512]{2,1,0:T(8,128)(2,1)} %bitcast.4), custom_call_target="tpu_custom_call" | custom-call | flops 28991029248 | bytes 18350080 | tf_op jit(solution)/shard_map/pallas_call | solution.py:371
  56.7 3.1 %copy.8 = bf16[2,8,128,512]{3,2,1,0:T(8,128)(2,1)} copy(bf16[2,8,128,512]{3,2,1,0:T(8,128)(2,1)} %shard_map.64) | data formatting | bytes 4194304

commit v2 on v1

--- a/solution.py
+++ b/solution.py
@@ -27,6 +27,7 @@
     prev,
     rim,
     wv,
+    line_buf,
     hid,
     acc,
     msg,
@@ -98,10 +99,29 @@
                     device_id_type=MESH,
                 )
 
+    def weight_copy(t, b):
+        return pltpu.make_async_copy(
+            weight.at[3 * t + b], wv.at[4 * t + (0, 1, 3)[b]], w_sem.at[3 * t + b]
+        )
+
+    def blend_weights(t):
+        for b in range(3):
+            weight_copy(t, b).wait()
+        size = 32
+
+        def body(i, _):
+            part = pl.ds(pl.multiple_of(i * size, size), size)
+            outer = wv[4 * t, part].astype(F32) + wv[4 * t + 3, part].astype(F32)
+            middle = wv[4 * t + 1, part].astype(F32)
+            wv[4 * t + 1, part] = (outer + middle).astype(jnp.bfloat16)
+            wv[4 * t + 2, part] = (outer - middle).astype(jnp.bfloat16)
+            return 0
+
+        lax.fori_loop(0, wv.shape[1] // size, body, 0)
+
     for t in (2, 1, 0):
         for b in range(3):
-            i = 3 * t + b
-            pltpu.make_async_copy(weight.at[i], wv.at[i], w_sem.at[i]).start()
+            weight_copy(t, b).start()
 
     start_of, end_of, total = [], [], jnp.int32(0)
     for r in range(requests):
@@ -208,6 +228,7 @@
     for side, has in row_sends:
         pl.when(has)(lambda side=side: rim_copy(2, side).start())
     pl.when(has_next)(lambda: frame_copy(1).start())
+    blend_weights(2)
 
     for k in range(1, members_a):
         copy_a(k).wait_send()
@@ -228,6 +249,8 @@
     for side, has in row_sends:
         pl.when(has & has_next)(lambda side=side: rim_copy(0, side).start())
     pl.when(has_next)(lambda: frame_copy(0).start())
+    blend_weights(1)
+    blend_weights(0)
     for k in range(1, reqs_n):
         copy_b(k).wait_send()
         other = (req + k) % reqs_n
@@ -265,7 +288,7 @@
             scale = jnp.where(inside, table[requests + r : requests + r + 1, :], scale)
         return mean, scale * gain[...] * 0.5, shift[...] * 0.5
 
-    def put_row(slot, row, read, coef):
+    def put_row(row, read, coef):
         mean, factor, offset = coef
         for c in range(0, channels, lane):
             part = slice(c, c + lane)
@@ -274,9 +297,9 @@
             y = h + h * jnp.tanh(h)
             left = jnp.where(first_col, y, pltpu.roll(y, 1, 0))
             right = jnp.where(last_col, y, pltpu.roll(y, cols - 1, 0))
-            hid[slot, row, :, c : c + lane] = left.astype(jnp.bfloat16)
-            hid[slot, row, :, channels + c : channels + c + lane] = y.astype(jnp.bfloat16)
-            hid[slot, row, :, 2 * channels + c : 2 * channels + c + lane] = right.astype(
+            line_buf[row, :, c : c + lane] = left.astype(jnp.bfloat16)
+            line_buf[row, :, channels + c : channels + c + lane] = y.astype(jnp.bfloat16)
+            line_buf[row, :, 2 * channels + c : 2 * channels + c + lane] = right.astype(
                 jnp.bfloat16
             )
 
@@ -284,7 +307,7 @@
         coef = coefficients(slot)
 
         def body(i, _):
-            put_row(slot, i + 1, lambda part: source[index, i, :, part], coef)
+            put_row(i + 1, lambda part: source[index, i, :, part], coef)
             return 0
 
         lax.fori_loop(0, rows, body, 0)
@@ -294,38 +317,55 @@
 
             @pl.when(has)
             def _():
-                put_row(slot, row, lambda part: rim[side, slot, :, part], coef)
+                put_row(row, lambda part: rim[side, slot, :, part], coef)
 
             @pl.when(jnp.logical_not(has))
             def _():
-                hid[slot, row] = hid[slot, 1 + edge]
+                line_buf[row] = line_buf[1 + edge]
+
+        def blend_rows(i, _):
+            for c in range(0, 3 * channels, lane):
+                part = slice(c, c + lane)
+                d0, d1, d2, d3 = [line_buf[2 * i + n, :, part] for n in range(4)]
+                hid[slot, 0, i, :, part] = d0 - d2
+                hid[slot, 1, i, :, part] = d1 + d2
+                hid[slot, 2, i, :, part] = d2 - d1
+                hid[slot, 3, i, :, part] = d1 - d3
+            return 0
+
+        lax.fori_loop(0, rows // 2, blend_rows, 0)
 
     def multiply(f, t, begin, end):
         source = jnp.maximum(first + f - 2 + t, start_at(f + 2)) - first + 2
 
-        def body(b, _):
-            if begin:
-                i = 3 * t + b
-                pltpu.make_async_copy(weight.at[i], wv.at[i], w_sem.at[i]).wait()
-            lhs = hid[source, pl.ds(b, rows)].reshape(rows * cols, 3 * channels)
-            acc[f] += jnp.dot(lhs, wv[3 * t + b], preferred_element_type=F32)
+        def body(k, _):
+            lhs = hid[source, k].reshape(rows // 2 * cols, 3 * channels)
+            term = jnp.dot(lhs, wv[4 * t + k], preferred_element_type=F32)
+            acc[f, k] = term if begin else acc[f, k] + term
             return 0
 
-        lax.fori_loop(0, 3, body, 0)
+        lax.fori_loop(0, 4, body, 0)
         if end:
-            value = own[f].reshape(rows * cols, channels).astype(F32) + acc[f] + bias[...]
-            own[f] = value.astype(jnp.bfloat16).reshape(rows, cols, channels)
+
+            def finish(i, _):
+                part = pl.ds(pl.multiple_of(i * cols, cols), cols)
+                m0, m1, m2, m3 = [acc[f, k, part] for k in range(4)]
+                for row, conv in ((2 * i, m0 + 0.5 * (m1 + m2)), (2 * i + 1, 0.5 * (m1 - m2) - m3)):
+                    value = own[f, row].astype(F32) + conv + bias[...]
+                    own[f, row] = value.astype(jnp.bfloat16)
+                return 0
+
+            lax.fori_loop(0, rows // 2, finish, 0)
             pltpu.make_async_copy(own.at[f], out.at[f], out_sem.at[f]).start()
 
     for side, has in row_recvs:
         pl.when(has)(lambda side=side: rim_copy(2, side).wait_recv())
     for f in range(frames):
         put_frame(f + 2, own, f)
-    acc[...] = jnp.zeros_like(acc)
 
     pairs = [(f, t) for f in range(frames) for t in (2, 1, 0)]
     order = sorted(pairs, key=lambda p: (max(0, 2 - p[0] - p[1]), -p[1], -p[0]))
-    seen, left = set(), {f: 3 for f in range(frames)}
+    left = {f: 3 for f in range(frames)}
     ready = 0
     for f, t in order:
         need = max(0, 2 - f - t)
@@ -342,8 +382,7 @@
                 put_frame(slot, prev, slot)
 
         left[f] -= 1
-        multiply(f, t, t not in seen, left[f] == 0)
-        seen.add(t)
+        multiply(f, t, left[f] == 2, left[f] == 0)
 
     for side, has in row_sends:
         pl.when(has)(lambda side=side: rim_copy(2, side).wait_send())
@@ -352,6 +391,18 @@
         pl.when(has_next)(lambda slot=slot: frame_copy(slot).wait_send())
     for f in range(frames):
         pltpu.make_async_copy(own.at[f], out.at[f], out_sem.at[f]).wait()
+
+
+def copy_kernel(source, target, sems):
+    frames, rows = source.shape[:2]
+
+    def each(act):
+        for f in range(frames):
+            for i in range(rows):
+                act(pltpu.make_async_copy(source.at[f, i], target.at[f, i], sems.at[f, i]))
+
+    each(lambda copy: copy.start())
+    each(lambda copy: copy.wait())
 
 
 def solution(mesh):
@@ -368,7 +419,7 @@
         whole = pl.BlockSpec(memory_space=pltpu.VMEM)
         anywhere = pl.BlockSpec(memory_space=pl.ANY)
         positions = frames * rows * cols
-        return pl.pallas_call(
+        result = pl.pallas_call(
             functools.partial(kernel, sizes),
             out_shape=jax.ShapeDtypeStruct(latents.shape, bf16),
             in_specs=[
@@ -384,9 +435,10 @@
                 pltpu.VMEM((frames, rows, cols, channels), bf16),
                 pltpu.VMEM((2, rows, cols, channels), bf16),
                 pltpu.VMEM((2, frames + 2, cols, channels), bf16),
-                pltpu.VMEM((9, 3 * channels, channels), bf16),
-                pltpu.VMEM((frames + 2, rows + 2, cols, 3 * channels), bf16),
-                pltpu.VMEM((frames, rows * cols, channels), F32),
+                pltpu.VMEM((12, 3 * channels, channels), bf16),
+                pltpu.VMEM((rows + 2, cols, 3 * channels), bf16),
+                pltpu.VMEM((frames + 2, 4, rows // 2, cols, 3 * channels), bf16),
+                pltpu.VMEM((frames, 4, rows // 2 * cols, channels), F32),
                 pltpu.VMEM((lines, 128), F32),
                 pltpu.VMEM((members, lines, 128), F32),
                 pltpu.VMEM((reqs_n, lines, 128), F32),
@@ -404,10 +456,10 @@
                 dma((2,)),
             ],
             compiler_params=pltpu.CompilerParams(
-                collective_id=0, has_side_effects=True, vmem_limit_bytes=56 * 1024 * 1024
+                collective_id=0, has_side_effects=True, vmem_limit_bytes=62 * 1024 * 1024
             ),
             cost_estimate=pl.CostEstimate(
-                flops=2 * positions * 3 * taps * channels * channels,
+                flops=2 * positions * 2 * taps * channels * channels,
                 bytes_accessed=2 * 3 * taps * channels * channels + 4 * positions * channels,
                 transcendentals=2 * positions * channels,
             ),
@@ -419,6 +471,13 @@
             conv_bias.reshape(1, channels),
             weight,
         )
+        return pl.pallas_call(
+            copy_kernel,
+            out_shape=jax.ShapeDtypeStruct(latents.shape, bf16),
+            in_specs=[anywhere],
+            out_specs=anywhere,
+            scratch_shapes=[dma((frames, rows))],
+        )(result)
 
     placed = (P(("req", "span"), "tile", None, None), P(), P(), P(), P(), P())
     return jax.shard_map(

time: 60 us -> 118 us (1.97)
  Pallas kernels: 56.7 us -> 117 us
  local copies, waits for them, and re-layouts: 3.1 us -> 0 us
    pallas_call x0 -> x1, Pallas kernels: none -> 64.8 us  [step(): pl.pallas_call(copy_kernel, out_shape=jax.ShapeDtypeStruct(latents.shape,...]
    pallas_call x1, Pallas kernels: 56.7 us -> 52.7 us  [step(): pl.pallas_call(functools.partial(kernel, sizes), out_shape=jax.ShapeDtype...]
    unnamed x1 -> x0, local copies, waits for them, and re-layouts: 3.1 us -> none
where the time goes in v2:
time: 118 us; the launch traced here: 117 us
  Pallas kernels  117 us (99%)
    pallas_call x1, Pallas kernels, step(): pl.pallas_call(copy_kernel, out_shape=jax.ShapeDtypeStruct(latents.shape,...  64.8 us
    pallas_call x1, Pallas kernels, step(): pl.pallas_call(functools.partial(kernel, sizes), out_shape=jax.ShapeDtype...  52.7 us

profile of v2, /device:TPU:15, one launch (start us, length us, event | category | flops | bytes accessed | tf_op | source)
XLA Modules:
  0.0 117.5 jit_solution(10043478588597247829)
XLA Ops:
  0.0 52.7 %shard_map.64.source = bf16[2,8,128,512]{3,2,1,0:T(8,128)(2,1)} custom-call(s32[4]{0:T(128)} %counts.1, bf16[2,8,128,512]{3,2,1,0:T(8,128)(2,1)} %lat.1, f32[1,512]{1,0:T(1,128)} %bitcast.5, f32[1,512]{1,0:T(1,128)} %bitcast.6, f32[1,512]{1,0:T(1,128)} %bitcast.7, bf16[9,1536,512]{2,1,0:T(8,128)(2,1)} %bitcast.4), custom_call_target="tpu_custom_call" | custom-call | flops 19327352832 | bytes 18350080 | tf_op jit(solution)/shard_map/pallas_call | solution.py:422
  52.7 64.8 %shard_map.65 = bf16[2,8,128,512]{3,2,1,0:T(8,128)(2,1)} custom-call(bf16[2,8,128,512]{3,2,1,0:T(8,128)(2,1)} %shard_map.64.source), custom_call_target="tpu_custom_call" | custom-call | tf_op jit(solution)/shard_map/pallas_call | solution.py:474

commit v3 on v1

--- a/solution.py
+++ b/solution.py
@@ -205,9 +205,6 @@
 
     for k in range(1, members_a):
         copy_a(k).start()
-    for side, has in row_sends:
-        pl.when(has)(lambda side=side: rim_copy(2, side).start())
-    pl.when(has_next)(lambda: frame_copy(1).start())
 
     for k in range(1, members_a):
         copy_a(k).wait_send()
@@ -225,6 +222,9 @@
     stat_b[req] = part
     for k in range(1, reqs_n):
         copy_b(k).start()
+    for side, has in row_sends:
+        pl.when(has)(lambda side=side: rim_copy(2, side).start())
+    pl.when(has_next)(lambda: frame_copy(1).start())
     for side, has in row_sends:
         pl.when(has & has_next)(lambda side=side: rim_copy(0, side).start())
     pl.when(has_next)(lambda: frame_copy(0).start())
@@ -354,6 +354,17 @@
         pltpu.make_async_copy(own.at[f], out.at[f], out_sem.at[f]).wait()
 
 
+def copy_kernel(source, target, held, in_sems, out_sems):
+    parts = held.shape[0]
+    for i in range(parts):
+        pltpu.make_async_copy(source.at[i], held.at[i], in_sems.at[i]).start()
+    for i in range(parts):
+        pltpu.make_async_copy(source.at[i], held.at[i], in_sems.at[i]).wait()
+        pltpu.make_async_copy(held.at[i], target.at[i], out_sems.at[i]).start()
+    for i in range(parts):
+        pltpu.make_async_copy(held.at[i], target.at[i], out_sems.at[i]).wait()
+
+
 def solution(mesh):
     sizes = (mesh.shape["req"], mesh.shape["tile"], mesh.shape["span"])
     reqs_n, tiles, spans = sizes
@@ -368,7 +379,7 @@
         whole = pl.BlockSpec(memory_space=pltpu.VMEM)
         anywhere = pl.BlockSpec(memory_space=pl.ANY)
         positions = frames * rows * cols
-        return pl.pallas_call(
+        result = pl.pallas_call(
             functools.partial(kernel, sizes),
             out_shape=jax.ShapeDtypeStruct(latents.shape, bf16),
             in_specs=[
@@ -419,6 +430,15 @@
             conv_bias.reshape(1, channels),
             weight,
         )
+        parts = (frames * rows // 2, 2, cols, channels)
+        return pl.pallas_call(
+            copy_kernel,
+            out_shape=jax.ShapeDtypeStruct(parts, bf16),
+            in_specs=[anywhere],
+            out_specs=anywhere,
+            scratch_shapes=[pltpu.VMEM(parts, bf16), dma((parts[0],)), dma((parts[0],))],
+            compiler_params=pltpu.CompilerParams(vmem_limit_bytes=58 * 1024 * 1024),
+        )(result.reshape(parts)).reshape(latents.shape)
 
     placed = (P(("req", "span"), "tile", None, None), P(), P(), P(), P(), P())
     return jax.shard_map(

time: 60 us -> 58.3 us (0.972)
  the two profiles are of different devices: /device:TPU:15 before, /device:TPU:1 now
where the time goes in v3:
time: 58.3 us; the launch traced here: 58.1 us
  Pallas kernels  58.1 us (100%)
    pallas_call x1, Pallas kernels, step(): pl.pallas_call(functools.partial(kernel, sizes), out_shape=jax.ShapeDtype...  55.7 us
    pallas_call x1, Pallas kernels, step(): pl.pallas_call(copy_kernel, out_shape=jax.ShapeDtypeStruct(parts, bf16),...  2.39 us

profile of v3, /device:TPU:1, one launch (start us, length us, event | category | flops | bytes accessed | tf_op | source)
XLA Modules:
  0.0 58.1 jit_solution(9090593857542518381)
XLA Ops:
  0.0 55.7 %shard_map.64 = bf16[2,8,128,512]{3,2,1,0:T(8,128)(2,1)} custom-call(s32[4]{0:T(128)} %counts.1, bf16[2,8,128,512]{3,2,1,0:T(8,128)(2,1)} %lat.1, f32[1,512]{1,0:T(1,128)} %bitcast.8, f32[1,512]{1,0:T(1,128)} %bitcast.9, f32[1,512]{1,0:T(1,128)} %bitcast.10, bf16[9,1536,512]{2,1,0:T(8,128)(2,1)} %bitcast.7), custom_call_target="tpu_custom_call" | custom-call | flops 28991029248 | bytes 18350080 | tf_op jit(solution)/shard_map/pallas_call | solution.py:382
  55.7 2.4 %shard_map.65 = bf16[8,2,128,512]{3,2,1,0:T(8,128)(2,1)} custom-call(bf16[8,2,128,512]{3,2,1,0:T(8,128)(2,1)} %bitcast.6), custom_call_target="tpu_custom_call" | custom-call | tf_op jit(solution)/shard_map/pallas_call | solution.py:434

commit v4 on v3

--- a/solution.py
+++ b/solution.py
@@ -10,7 +10,6 @@
 GROUPS = 32
 EPSILON = 1e-06
 MESH = pl.DeviceIdType.MESH
-HIGHEST = lax.Precision.HIGHEST
 F32 = jnp.float32
 
 
@@ -140,15 +139,22 @@
                 line = line + jnp.where(member(f + 2, r), per_frame[f][which], 0.0)
             table[which * requests + r : which * requests + r + 1, :] = line
     lanes = msg.shape[1]
-    to_group = (
-        lax.broadcasted_iota(jnp.int32, (channels, lanes), 0) // per_group
-        == lax.broadcasted_iota(jnp.int32, (channels, lanes), 1)
-    ).astype(F32)
-    from_group = (
-        lax.broadcasted_iota(jnp.int32, (lanes, channels), 1) // per_group
-        == lax.broadcasted_iota(jnp.int32, (lanes, channels), 0)
-    ).astype(F32)
-    msg[...] = jnp.dot(table[...], to_group, precision=HIGHEST, preferred_element_type=F32)
+    pieces = channels // lanes
+    spot = lax.broadcasted_iota(jnp.int32, (msg.shape[0], lanes), 1)
+
+    def spread_sum(x, width):
+        k = 1
+        while k < width:
+            after, before = pltpu.roll(x, lanes - k, 1), pltpu.roll(x, k, 1)
+            x = x + jnp.where((spot & k) == 0, after, before)
+            k *= 2
+        return x
+
+    packed = jnp.zeros((msg.shape[0], lanes), F32)
+    for v in range(pieces):
+        group = spread_sum(table[:, v * lanes : (v + 1) * lanes], per_group)
+        packed = jnp.where(spot % pieces == v, group, packed)
+    msg[...] = packed
     stat_a[me_a] = msg[...]
 
     near = has_up.astype(jnp.int32) + has_down.astype(jnp.int32)
@@ -205,6 +211,8 @@
 
     for k in range(1, members_a):
         copy_a(k).start()
+    for side, has in row_sends:
+        pl.when(has)(lambda side=side: rim_copy(2, side).start())
 
     for k in range(1, members_a):
         copy_a(k).wait_send()
@@ -222,8 +230,6 @@
     stat_b[req] = part
     for k in range(1, reqs_n):
         copy_b(k).start()
-    for side, has in row_sends:
-        pl.when(has)(lambda side=side: rim_copy(2, side).start())
     pl.when(has_next)(lambda: frame_copy(1).start())
     for side, has in row_sends:
         pl.when(has & has_next)(lambda side=side: rim_copy(0, side).start())
@@ -250,7 +256,9 @@
     for r in range(requests):
         msg[r : r + 1, :] = lines[r][0]
         msg[requests + r : requests + r + 1, :] = lines[r][1]
-    table[...] = jnp.dot(msg[...], from_group, precision=HIGHEST, preferred_element_type=F32)
+    for v in range(pieces):
+        chosen = jnp.where(spot % pieces == v, msg[...], 0.0)
+        table[:, v * lanes : (v + 1) * lanes] = spread_sum(chosen, pieces)
 
     lane = min(128, channels)
     first_col = lax.broadcasted_iota(jnp.int32, (cols, lane), 0) == 0
@@ -280,7 +288,7 @@
                 jnp.bfloat16
             )
 
-    def put_frame(slot, source, index):
+    def put_inner(slot, source, index):
         coef = coefficients(slot)
 
         def body(i, _):
@@ -288,6 +296,9 @@
             return 0
 
         lax.fori_loop(0, rows, body, 0)
+
+    def put_edges(slot):
+        coef = coefficients(slot)
         for side, has in row_recvs:
             row = 0 if side == 0 else rows + 1
             edge = 0 if side == 0 else rows - 1
@@ -300,28 +311,35 @@
             def _():
                 hid[slot, row] = hid[slot, 1 + edge]
 
-    def multiply(f, t, begin, end):
+    def multiply(f, t, begin, opens, end):
         source = jnp.maximum(first + f - 2 + t, start_at(f + 2)) - first + 2
 
-        def body(b, _):
+        def product(b):
             if begin:
                 i = 3 * t + b
                 pltpu.make_async_copy(weight.at[i], wv.at[i], w_sem.at[i]).wait()
             lhs = hid[source, pl.ds(b, rows)].reshape(rows * cols, 3 * channels)
-            acc[f] += jnp.dot(lhs, wv[3 * t + b], preferred_element_type=F32)
+            return jnp.dot(lhs, wv[3 * t + b], preferred_element_type=F32)
+
+        def body(b, _):
+            acc[f] += product(b)
             return 0
 
-        lax.fori_loop(0, 3, body, 0)
+        if opens:
+            acc[f] = product(0)
+        lax.fori_loop(1 if opens else 0, 2 if end else 3, body, 0)
         if end:
-            value = own[f].reshape(rows * cols, channels).astype(F32) + acc[f] + bias[...]
+            value = own[f].reshape(rows * cols, channels).astype(F32) + bias[...]
+            value = value + (acc[f] + product(2))
             own[f] = value.astype(jnp.bfloat16).reshape(rows, cols, channels)
             pltpu.make_async_copy(own.at[f], out.at[f], out_sem.at[f]).start()
 
+    for f in range(frames):
+        put_inner(f + 2, own, f)
     for side, has in row_recvs:
         pl.when(has)(lambda side=side: rim_copy(2, side).wait_recv())
     for f in range(frames):
-        put_frame(f + 2, own, f)
-    acc[...] = jnp.zeros_like(acc)
+        put_edges(f + 2)
 
     pairs = [(f, t) for f in range(frames) for t in (2, 1, 0)]
     order = sorted(pairs, key=lambda p: (max(0, 2 - p[0] - p[1]), -p[1], -p[0]))
@@ -339,10 +357,11 @@
                 if ready == 1:
                     for side, has in row_recvs:
                         pl.when(has)(lambda side=side: rim_copy(0, side).wait_recv())
-                put_frame(slot, prev, slot)
+                put_inner(slot, prev, slot)
+                put_edges(slot)
 
         left[f] -= 1
-        multiply(f, t, t not in seen, left[f] == 0)
+        multiply(f, t, t not in seen, left[f] == 2, left[f] == 0)
         seen.add(t)
 
     for side, has in row_sends:

time: 58.3 us -> 54.8 us (0.940)
  Pallas kernels: 58.1 us -> 54.6 us
    pallas_call x1, Pallas kernels: 55.7 us -> 52.2 us  [step(): pl.pallas_call(functools.partial(kernel, sizes), out_shape=jax.ShapeDtype...]
where the time goes in v4:
time: 54.8 us; the launch traced here: 54.6 us
  Pallas kernels  54.6 us (100%)
    pallas_call x1, Pallas kernels, step(): pl.pallas_call(functools.partial(kernel, sizes), out_shape=jax.ShapeDtype...  52.2 us
    pallas_call x1, Pallas kernels, step(): pl.pallas_call(copy_kernel, out_shape=jax.ShapeDtypeStruct(parts, bf16),...  2.39 us

profile of v4, /device:TPU:1, one launch (start us, length us, event | category | flops | bytes accessed | tf_op | source)
XLA Modules:
  0.0 54.6 jit_solution(15281994994981675682)
XLA Ops:
  0.0 52.2 %shard_map.64 = bf16[2,8,128,512]{3,2,1,0:T(8,128)(2,1)} custom-call(s32[4]{0:T(128)} %counts.1, bf16[2,8,128,512]{3,2,1,0:T(8,128)(2,1)} %lat.1, f32[1,512]{1,0:T(1,128)} %bitcast.8, f32[1,512]{1,0:T(1,128)} %bitcast.9, f32[1,512]{1,0:T(1,128)} %bitcast.10, bf16[9,1536,512]{2,1,0:T(8,128)(2,1)} %bitcast.7), custom_call_target="tpu_custom_call" | custom-call | flops 28991029248 | bytes 18350080 | tf_op jit(solution)/shard_map/pallas_call | solution.py:401
  52.2 2.4 %shard_map.65 = bf16[8,2,128,512]{3,2,1,0:T(8,128)(2,1)} custom-call(bf16[8,2,128,512]{3,2,1,0:T(8,128)(2,1)} %bitcast.6), custom_call_target="tpu_custom_call" | custom-call | tf_op jit(solution)/shard_map/pallas_call | solution.py:453

commit v5 on v4

--- a/solution.py
+++ b/solution.py
@@ -97,9 +97,8 @@
                     device_id_type=MESH,
                 )
 
-    for t in (2, 1, 0):
-        for b in range(3):
-            i = 3 * t + b
+    def load_weights(t):
+        for i in range(3 * t, 3 * t + 3):
             pltpu.make_async_copy(weight.at[i], wv.at[i], w_sem.at[i]).start()
 
     start_of, end_of, total = [], [], jnp.int32(0)
@@ -230,10 +229,13 @@
     stat_b[req] = part
     for k in range(1, reqs_n):
         copy_b(k).start()
+    load_weights(2)
+    load_weights(1)
     pl.when(has_next)(lambda: frame_copy(1).start())
     for side, has in row_sends:
         pl.when(has & has_next)(lambda side=side: rim_copy(0, side).start())
     pl.when(has_next)(lambda: frame_copy(0).start())
+    load_weights(0)
     for k in range(1, reqs_n):
         copy_b(k).wait_send()
         other = (req + k) % reqs_n

time: 54.8 us -> 54.8 us (level)
  no operation moved by 1% of the time
where the time goes in v5:
time: 54.8 us; the launch traced here: 54.6 us
  Pallas kernels  54.6 us (100%)
    pallas_call x1, Pallas kernels, step(): pl.pallas_call(functools.partial(kernel, sizes), out_shape=jax.ShapeDtype...  52.2 us
    pallas_call x1, Pallas kernels, step(): pl.pallas_call(copy_kernel, out_shape=jax.ShapeDtypeStruct(parts, bf16),...  2.39 us

profile of v5, /device:TPU:1, one launch (start us, length us, event | category | flops | bytes accessed | tf_op | source)
XLA Modules:
  0.0 54.6 jit_solution(2344509001617601248)
XLA Ops:
  0.0 52.2 %shard_map.64 = bf16[2,8,128,512]{3,2,1,0:T(8,128)(2,1)} custom-call(s32[4]{0:T(128)} %counts.1, bf16[2,8,128,512]{3,2,1,0:T(8,128)(2,1)} %lat.1, f32[1,512]{1,0:T(1,128)} %bitcast.8, f32[1,512]{1,0:T(1,128)} %bitcast.9, f32[1,512]{1,0:T(1,128)} %bitcast.10, bf16[9,1536,512]{2,1,0:T(8,128)(2,1)} %bitcast.7), custom_call_target="tpu_custom_call" | custom-call | flops 28991029248 | bytes 18350080 | tf_op jit(solution)/shard_map/pallas_call | solution.py:403
  52.2 2.4 %shard_map.65 = bf16[8,2,128,512]{3,2,1,0:T(8,128)(2,1)} custom-call(bf16[8,2,128,512]{3,2,1,0:T(8,128)(2,1)} %bitcast.6), custom_call_target="tpu_custom_call" | custom-call | tf_op jit(solution)/shard_map/pallas_call | solution.py:455
